TPU v7x, 256 devices: a whole 4x4x8 slice. The times are simulated.
256 devices in a mesh: tgroup: 8 (over z), chan: 32 (over y, x, core).
Axes of the slice: x: 4, y: 4, z: 8, core: 2. Of those that a mesh axis runs over, the one named last changes fastest.
Arguments:
- raw_strain: float32 [32768, 10240], P(('tgroup', 'chan')), may hold values from -6 to 6
- whitening_taps: float32 [255], replicated, may hold values from -0.375 to 0.375
- first_block: int32 [64], P('chan'), may hold values from 0 to 39, as said below
- pair_owner: int32 [512, 1], P('chan'), may hold values from 0 to 7; in each aligned block of 16 rows (0 to 15, 16 to 31, ...) at most 5 rows name the same one
Outputs:
- stacks: float32 [1280, 8, 8, 1001], P(('tgroup', 'chan'))
Inputs may be any that keep to these rules, and one draw needn't show every extreme that they name: `first_block`: each chan index lists 2 stripes; its first stripe starts within the last 7 of its 40 blocks; chan index 0 lists block 39 first and block 0 second. `pair_owner`: pair blocks are ordered by chan index, stripe, then partner offset. Among the 16 pair blocks of one chan index at most 5 share an owner, and exactly 5 do in some chan index.
All inputs are finite; a program needn't handle non-finite values.
Results may differ from a plain program's by a relative error of at most 0.02.
Values may be sent and summed in bfloat16 or wider, within the bound.
A program may use at most 128 MiB of HBM per device.

v0:
```python
import math

import jax
import jax.numpy as jnp
from jax import lax
from jax.sharding import PartitionSpec as P

MAXLAG = 500
CB = 8
K = 8
STRIPES = 2
SLOTS = 5


def from_behind(value, axis, steps):
    count = lax.axis_size(axis)
    first, last = (max(0, -steps), min(count, count - steps))
    return lax.ppermute(value, axis, [(source, source + steps) for source in range(first, last)])


def fir_matrix(whitening_taps, out_rows):
    padded = jnp.concatenate([whitening_taps, jnp.zeros((2 * out_rows,), whitening_taps.dtype)])
    length = padded.shape[0]
    tiled_taps = jnp.tile(padded, out_rows + 1)[: out_rows * (length - 2)]
    return tiled_taps.reshape(out_rows, length - 2)


def whiten(padded, whitening_taps):
    row_count = padded.shape[0] - whitening_taps.shape[0] + 1
    out_rows = min(256, row_count // 2)
    blocks = row_count // (2 * out_rows)
    matrix = fir_matrix(whitening_taps, out_rows)
    span_cols = matrix.shape[1]
    starts = jnp.arange(blocks, dtype=jnp.int32) * (2 * out_rows)

    def take_window(offset_row):
        return lax.dynamic_slice_in_dim(padded, offset_row, span_cols, 0)

    windows = jax.vmap(take_window)(starts)
    result = jnp.einsum("jq,bqc->cbj", matrix, windows, precision=lax.Precision.HIGHEST)
    return result.reshape(result.shape[0], blocks * out_rows).astype(jnp.bfloat16)


def correlate(source, offset_row, factor):
    lag_count = 2 * MAXLAG + 1
    lag_block = 128
    lag_blocks = (lag_count + lag_block - 1) // lag_block
    sample_count = source.shape[1]
    span_width = sample_count + lag_block
    leading = lax.dynamic_slice_in_dim(source, offset_row, CB, 0)
    partners = lax.dynamic_slice_in_dim(source, offset_row, K * CB, 0)
    lead_padded = jnp.pad(leading, ((0, 0), (lag_block - 1, lag_block + 1)))

    def shifted_copy(shift_count):
        return lax.dynamic_slice_in_dim(lead_padded, lag_block - 1 - shift_count, span_width, 1)

    shifted = jax.vmap(shifted_copy)(jnp.arange(lag_block, dtype=jnp.int32))
    extra_right = MAXLAG + lag_blocks * lag_block - lag_count + 1
    partner_padded = jnp.pad(partners, ((0, 0), (MAXLAG, extra_right)))
    windows = jnp.stack(
        [
            partner_padded[:, block_index * lag_block : block_index * lag_block + span_width]
            for block_index in range(lag_blocks)
        ],
        0,
    )
    summed = jnp.einsum("raj,nbj->banr", shifted, windows, preferred_element_type=jnp.float32)
    summed = summed.reshape(K * CB, CB, lag_blocks * lag_block)[:, :, :lag_count]
    scaled = (summed * factor).astype(jnp.bfloat16)
    return scaled.reshape(K, CB, CB, lag_count).transpose(0, 2, 1, 3)


def local(raw_strain, whitening_taps, first_block, pair_owner):
    half_taps = (whitening_taps.shape[0] - 1) // 2
    chan_count = lax.axis_size("chan")
    local_rows = raw_strain.shape[0]
    grouped = raw_strain.reshape(local_rows, chan_count, raw_strain.shape[1] // chan_count)
    series = lax.all_to_all(
        grouped.astype(jnp.bfloat16), "chan", split_axis=1, concat_axis=0, tiled=True
    ).astype(grouped.dtype)[:, 0, :]
    padded = jnp.pad(series, ((half_taps, half_taps), (0, 0)))
    filtered = whiten(padded, whitening_taps)
    rim_rows = from_behind(filtered[: (K - 1) * CB], "chan", -1)
    extended = jnp.concatenate([filtered, rim_rows], 0)
    offsets = [first_block[stripe] * CB for stripe in range(STRIPES)]
    factor = 1.0 / math.sqrt(extended.shape[1])
    lag_count = 2 * MAXLAG + 1
    partial_value = jnp.concatenate(
        [correlate(extended, offset_row, factor) for offset_row in offsets], 0
    )
    pair_count = partial_value.shape[0]
    flat_partial = partial_value.reshape(pair_count, CB * CB * lag_count)
    group_count = lax.axis_size("tgroup")
    owners_vec = pair_owner[:, 0]
    owner_hot = (owners_vec[:, None] == jnp.arange(group_count, dtype=jnp.int32)[None, :]).astype(
        jnp.int32
    )
    earlier = (
        jnp.arange(pair_count, dtype=jnp.int32)[None, :]
        < jnp.arange(pair_count, dtype=jnp.int32)[:, None]
    ).astype(jnp.int32)
    before_count = jnp.dot(earlier, owner_hot)
    slot_index = jnp.sum(before_count * owner_hot, 1)
    target = owners_vec * SLOTS + slot_index
    placement = jnp.arange(group_count * SLOTS, dtype=jnp.int32)[:, None] == target[None, :]
    placement_half = placement.astype(jnp.bfloat16)
    mine = lax.psum_scatter(
        jnp.dot(placement_half, flat_partial, preferred_element_type=jnp.float32).astype(
            jnp.bfloat16
        ),
        "tgroup",
        scatter_dimension=0,
        tiled=True,
    ).astype(jnp.float32)
    return mine.reshape(SLOTS, CB, CB, lag_count)


def solution(mesh):
    in_specs = (P(("tgroup", "chan"), None), P(), P("chan"), P("chan", None))
    out_specs = P(("tgroup", "chan"), None, None, None)
    return jax.shard_map(local, mesh=mesh, in_specs=in_specs, out_specs=out_specs, check_vma=False)
```

profile of v0, /device:TPU:56, one launch (start us, length us, event | category | flops | bytes accessed | tf_op | source)
XLA Modules:
  0.0 775.5 jit_solution(11667853301549032144)
XLA Ops:
  6.5 4.9 copy.31
  11.4 7.5 all-to-all-start
  21.1 1.5 tile.10
  23.8 1.6 reshape.152
  25.6 26.3 %all-to-all-done = bf16[128,32,320]{0,2,1:T(8,128)(2,1)S(1)} async-done(((bf16[128,32,320]{0,2,1:T(8,128)(2,1)}), bf16[128,32,320]{0,2,1:T(8,128)(2,1)S(1)}, u32[]{:S(2)}, u32[]{:S(2)}) %all-to-all-start) | async-done | bytes 2621472 | tf_op jit(solution)/shard_map/all_to_all | solution.py:78
  51.9 1.7 copy.32
  54.8 2.7 pad.24
  57.6 30.0 %while.3 = (s32[]{:T(128)}, bf16[4350,320]{0,1:T(8,128)(2,1)}, s32[8,2]{0,1:T(2,128)S(1)}, bf16[8,765,320]{2,1,0:T(8,128)(2,1)}, s32[]{:T(128)}) while((s32[]{:T(128)}, bf16[4350,320]{0,1:T(8,128)(2,1)}, s32[8,2]{0,1:T(2,128)S(1)}, bf16[8,765,320]{2,1,0:T(8,128)(2,1)}, s32[]{:T(128)}) %tuple.44), condition=%wide.while_cond, body=%wide.while_body.sunk | while | flops 2 | bytes 3037929 | solution.py:37
  58.2 1.9 constant_dynamic-slice_fusion.13
  62.0 1.9 constant_dynamic-slice_fusion.13
  65.7 1.9 constant_dynamic-slice_fusion.13
  69.5 1.9 constant_dynamic-slice_fusion.13
  73.2 1.9 constant_dynamic-slice_fusion.13
  77.0 1.9 constant_dynamic-slice_fusion.13
  80.8 1.9 constant_dynamic-slice_fusion.13
  84.5 1.9 constant_dynamic-slice_fusion.13
  87.6 7.5 convolution_convert_fusion.1
  95.2 2.6 collective-permute-start
  98.0 3.2 collective-permute-done
  101.3 2.3 broadcast.106.clone
  103.7 246.9 %while.5 = (s32[]{:T(128)}, bf16[8,2304]{1,0:T(8,128)(2,1)S(1)}, s32[128,2]{0,1:T(2,128)S(1)}, bf16[128,8,2176]{2,1,0:T(8,128)(2,1)}, s32[]{:T(128)}) while((s32[]{:T(128)}, bf16[8,2304]{1,0:T(8,128)(2,1)S(1)}, s32[128,2]{0,1:T(2,128)S(1)}, bf16[128,8,2176]{2,1,0:T(8,128)(2,1)}, s32[]{:T(128)}) %tuple.47), condition=%wide.while_cond.2, body=%wide.while_body.2.sunk | while | flops 2 | bytes 70245 | solution.py:55
  113.9 1.4 bitcast_dynamic-update-slice_fusion.8
  123.6 1.3 bitcast_dynamic-update-slice_fusion.8
  139.0 1.3 bitcast_dynamic-update-slice_fusion.8
  140.9 1.3 bitcast_dynamic-update-slice_fusion.8
  142.8 1.3 bitcast_dynamic-update-slice_fusion.8
  152.5 1.3 bitcast_dynamic-update-slice_fusion.8
  200.7 1.3 bitcast_dynamic-update-slice_fusion.8
  204.6 1.3 bitcast_dynamic-update-slice_fusion.8
  218.1 1.4 bitcast_dynamic-update-slice_fusion.8
  235.4 1.3 bitcast_dynamic-update-slice_fusion.8
  248.9 1.3 bitcast_dynamic-update-slice_fusion.8
  264.3 1.3 bitcast_dynamic-update-slice_fusion.8
  268.2 1.4 bitcast_dynamic-update-slice_fusion.8
  283.6 1.4 bitcast_dynamic-update-slice_fusion.8
  302.9 1.3 bitcast_dynamic-update-slice_fusion.8
  352.9 2.6 fusion.15
  356.8 1.5 reshape.88
  358.3 1.8 fusion.8
  360.8 2.3 broadcast.106.clone.1
  363.2 246.9 %while.4 = (s32[]{:T(128)}, bf16[8,2304]{1,0:T(8,128)(2,1)S(1)}, s32[128,2]{0,1:T(2,128)S(1)}, bf16[128,8,2176]{2,1,0:T(8,128)(2,1)}, s32[]{:T(128)}) while((s32[]{:T(128)}, bf16[8,2304]{1,0:T(8,128)(2,1)S(1)}, s32[128,2]{0,1:T(2,128)S(1)}, bf16[128,8,2176]{2,1,0:T(8,128)(2,1)}, s32[]{:T(128)}) %tuple.55), condition=%wide.while_cond.1, body=%wide.while_body.1.sunk | while | flops 2 | bytes 70245 | solution.py:55
  373.4 1.4 bitcast_dynamic-update-slice_fusion.7
  383.0 1.3 bitcast_dynamic-update-slice_fusion.7
  398.4 1.3 bitcast_dynamic-update-slice_fusion.7
  400.4 1.3 bitcast_dynamic-update-slice_fusion.7
  402.3 1.3 bitcast_dynamic-update-slice_fusion.7
  412.0 1.3 bitcast_dynamic-update-slice_fusion.7
  460.2 1.3 bitcast_dynamic-update-slice_fusion.7
  464.0 1.3 bitcast_dynamic-update-slice_fusion.7
  477.6 1.4 bitcast_dynamic-update-slice_fusion.7
  494.9 1.3 bitcast_dynamic-update-slice_fusion.7
  508.4 1.3 bitcast_dynamic-update-slice_fusion.7
  523.8 1.3 bitcast_dynamic-update-slice_fusion.7
  527.7 1.4 bitcast_dynamic-update-slice_fusion.7
  543.1 1.4 bitcast_dynamic-update-slice_fusion.7
  562.4 1.3 bitcast_dynamic-update-slice_fusion.7
  616.0 5.6 fusion.10
  622.8 1.5 reshape.86
  624.3 1.8 fusion.9
  627.0 3.3 reshape.90
  630.3 5.3 convolution_convert_fusion
  637.5 127.2 %all-reduce.11.cloned.1.call-done = bf16[40,64064]{1,0:T(8,128)(2,1)} async-done(((bf16[40,64064]{1,0:T(8,128)(2,1)}), bf16[40,64064]{1,0:T(8,128)(2,1)}) %all-reduce.11.cloned.1.call-update) | async-done | bytes 5125136
  764.8 1.8 dynamic-slice_convert_fusion
  766.6 2.1 reshape.151
  (826 shorter events, 484.9 us)
Async XLA Ops:
  11.4 7.6 copy-start.2
  11.4 9.6 %copy-start.3 = (f32[255]{0:T(256)S(1)}, f32[255]{0:T(256)}, u32[]{:S(2)}) copy-start(f32[255]{0:T(256)} %param.5) | copy-start | bytes 3064
  11.4 40.4 %all-to-all-start = ((bf16[128,32,320]{0,2,1:T(8,128)(2,1)}), bf16[128,32,320]{0,2,1:T(8,128)(2,1)S(1)}, u32[]{:S(2)}, u32[]{:S(2)}) async-start(bf16[128,32,320]{0,2,1:T(8,128)(2,1)} %bitcast.155), calls=%async_computation | async-start | bytes 5242880 | tf_op jit(solution)/shard_map/all_to_all | solution.py:78
  18.9 745.8 %all-reduce.11.cloned.1.call-start = ((), (), s32[]{:S(2)}) async-start(), calls=%async_computation.1 | async-start | bytes 10260480
  21.1 4.3 copy-start.4
  57.6 30.0 %copy-start.1 = (f32[256,765,1]{1,0,2:T(8,128)S(1)}, f32[256,765,1]{1,0,2:T(8,128)}, u32[]{:S(2)}) copy-start(f32[256,765,1]{1,0,2:T(8,128)} %reshape.152) | copy-start | bytes 2350084
  95.2 5.9 collective-permute-start
  350.5 2.4 copy-start
  635.6 0.7 copy-start.5
Sparse Core Ops, SparseCore 0:
  635.8 128.9 all-reduce.10
where the time goes:
time: 783 us; the launch traced here: 776 us
  local copies, waits for them, and re-layouts  566 us (72%)
  waiting for transfers between devices  157 us (20%)
  matrix products  21.1 us (3%)
  between operations  15.7 us (2%)
  starting transfers between devices  10.1 us (1%)
    gather x808, local copies, waits for them, and re-layouts  523 us
    unnamed x2, waiting for transfers between devices  127 us
    all_to_all x1, waiting for transfers between devices, local(): lax.all_to_all(grouped.astype(jnp.bfloat16), 'chan', split_axis=1, concat...  26.3 us
    unnamed x32, local copies, waits for them, and re-layouts  19.6 us
  transfers between devices with their start and end apart: 3, of which 3 were waited for; matrix products, arithmetic and copies ran while one was open for 1% of the time, Pallas kernels for 0%

commit v1 on v0

v1 whole, which is shorter than its diff:
```python
import math

import jax
import jax.numpy as jnp
from jax import lax
from jax.experimental import pallas as pl
from jax.experimental.pallas import tpu as pltpu
from jax.sharding import PartitionSpec as P

MESH = pl.DeviceIdType.MESH
MAXLAG = 500
LAGS = 1001
CB = 8
K = 8
STRIPES = 2
SLOTS = 5
TAPS = 255
NG = 8
NC = 32
CPD = 320
CHANNELS = 10240
ROWS = 128
TS = 4096
TD = 2048
PAIRS = STRIPES * K
WIDE = CHANNELS + 128
FB = 256
FW = 768
R = 32
KL = TD + 128
SPAN = 384
QW = TD + 1024
F32 = jnp.float32
BF = jnp.bfloat16


def chan_copy(send_ref, x_ref, send_sem, recv_sem, dst, src):
    return pltpu.make_async_remote_copy(
        src_ref=send_ref.at[dst],
        dst_ref=x_ref.at[1 + src],
        send_sem=send_sem.at[dst],
        recv_sem=recv_sem.at[src],
        device_id={"chan": dst},
        device_id_type=MESH,
    )


def first_copy(fb_ref, table_ref, send_sem, recv_sem, dst, src):
    return pltpu.make_async_remote_copy(
        src_ref=fb_ref.at[0],
        dst_ref=table_ref.at[src],
        send_sem=send_sem.at[dst],
        recv_sem=recv_sem.at[src],
        device_id={"chan": dst},
        device_id_type=MESH,
    )


def group_copy(src_ref, dst_ref, send_sem, recv_sem, dst, src):
    return pltpu.make_async_remote_copy(
        src_ref=src_ref,
        dst_ref=dst_ref.at[src],
        send_sem=send_sem.at[dst],
        recv_sem=recv_sem.at[src],
        device_id={"tgroup": dst},
        device_id_type=MESH,
    )


def kernel(
    raw_ref, taps_ref, fb_ref, owner_ref, out_ref,
    raw_v, by_chan, table_v, fb_v, send_v, x_v, filt, zsend, zrecv, leads, lead_f, shifted, windows, acc,
    raw_sem, fsend, frecv, csend, crecv, zs, zr, ls, lr,
):
    me_c = lax.axis_index("chan")
    me_g = lax.axis_index("tgroup")

    barrier = pltpu.get_barrier_semaphore()

    def greet_chan(d, carry):
        pl.semaphore_signal(barrier, inc=1, device_id={"chan": lax.rem(me_c + d, NC)}, device_id_type=MESH)
        return carry

    def greet_group(d, carry):
        pl.semaphore_signal(barrier, inc=1, device_id={"tgroup": lax.rem(me_g + d, NG)}, device_id_type=MESH)
        return carry

    lax.fori_loop(1, NC, greet_chan, 0)
    lax.fori_loop(1, NG, greet_group, 0)

    raw_in = pltpu.make_async_copy(raw_ref, raw_v, raw_sem)
    raw_in.start()
    lane = lax.broadcasted_iota(jnp.int32, (8, 128), 1)
    fb_v[0] = jnp.where(lane == 0, fb_ref[0], jnp.where(lane == 1, fb_ref[1], 0))
    table_v[me_c] = fb_v[0]
    by_chan[pl.ds(CHANNELS, 128)] = jnp.zeros((128, ROWS), BF)
    x_v[0] = jnp.zeros((128, ROWS), BF)
    x_v[NC + 1] = jnp.zeros((128, ROWS), BF)
    lead_f[:, pl.ds(TD, 128)] = jnp.zeros((STRIPES * CB, 128), F32)
    acc[...] = jnp.zeros_like(acc)
    pl.semaphore_wait(barrier, NC + NG - 2)

    def send_first(d, carry):
        first_copy(fb_v, table_v, fsend, frecv, lax.rem(me_c + d, NC), me_c).start()
        return carry

    def wait_first(d, carry):
        first_copy(fb_v, table_v, fsend, frecv, lax.rem(me_c + d, NC), lax.rem(me_c + NC - d, NC)).wait_recv()
        return carry

    def wait_first_sent(d, carry):
        first_copy(fb_v, table_v, fsend, frecv, lax.rem(me_c + d, NC), me_c).wait_send()
        return carry

    lax.fori_loop(1, NC, send_first, 0)
    raw_in.wait()

    def turn_over(i, carry):
        at = pl.multiple_of(i * 128, 128)
        by_chan[pl.ds(at, 128)] = raw_v[:, pl.ds(at, 128)].T.astype(BF)
        return carry

    lax.fori_loop(0, CHANNELS // 128, turn_over, 0)

    band = pltpu.roll(jnp.broadcast_to(taps_ref[...], (FB, FW)), 0, 1, stride=2, stride_axis=0)
    band_hi = band.astype(BF)
    band_lo = (band - band_hi.astype(F32)).astype(BF)

    owners = [owner_ref[q, 0] for q in range(PAIRS)]
    slots = []
    for q in range(PAIRS):
        count = jnp.int32(0)
        for earlier in range(q):
            count = count + jnp.where(owners[earlier] == owners[q], 1, 0)
        slots.append(count)
    lane_row = lax.broadcasted_iota(jnp.int32, (1, 128), 1)
    target = jnp.zeros((1, 128), jnp.int32)
    for q in range(PAIRS):
        target = jnp.where(lane_row // CB == q, owners[q] * SLOTS + slots[q], target)
    stripe_of = []
    for s in range(SLOTS):
        value = jnp.int32(0)
        for q in range(K, PAIRS):
            value = value + jnp.where((owners[q] == me_g) & (slots[q] == s), 1, 0)
        stripe_of.append(value)

    lax.fori_loop(1, NC, wait_first, 0)

    pick_row = lax.broadcasted_iota(jnp.int32, (128, SPAN), 0)
    pick_col = lax.broadcasted_iota(jnp.int32, (128, SPAN), 1)
    offset = pick_col - pick_row % (K * CB)

    def packed(dst):
        firsts = table_v[dst]
        wanted = jnp.where(pick_row < K * CB, firsts[:1, :1], firsts[:1, 1:2]) * CB
        source = by_chan[pl.ds(pl.multiple_of(dst * CPD, K * CB), SPAN)]
        chosen = jnp.where(offset == wanted, 1.0, 0.0).astype(BF)
        return jnp.dot(chosen, source, preferred_element_type=F32).astype(BF)

    def send_packed(d, carry):
        dst = lax.rem(me_c + d, NC)
        send_v[dst] = packed(dst)
        chan_copy(send_v, x_v, csend, crecv, dst, me_c).start()
        return carry

    lax.fori_loop(1, NC, send_packed, 0)
    x_v[1 + me_c] = packed(me_c)

    def wait_packed(d, carry):
        chan_copy(send_v, x_v, csend, crecv, lax.rem(me_c + d, NC), lax.rem(me_c + NC - d, NC)).wait_recv()
        return carry

    lax.fori_loop(1, NC, wait_packed, 0)

    for block in range(TD // FB):
        window = jnp.concatenate([x_v[4 * block + part] for part in range(FW // ROWS)], 1)
        y = sum(
            lax.dot_general(window, term, (((1,), (1,)), ((), ())), preferred_element_type=F32)
            for term in (band_hi, band_lo)
        )
        filt[:, pl.ds(block * FB, FB)] = y.astype(BF)

    rows = NG * SLOTS * CB
    row_id = lax.broadcasted_iota(jnp.int32, (rows, 128), 0)
    col_id = lax.broadcasted_iota(jnp.int32, (rows, 128), 1)
    pick = (jnp.broadcast_to(target, (rows, 128)) == row_id // CB) & (row_id % CB == col_id % CB)
    chosen = jnp.dot(jnp.where(pick, 1.0, 0.0).astype(BF), filt[...], preferred_element_type=F32)
    for owner in range(NG):
        part = chosen[owner * SLOTS * CB:(owner + 1) * SLOTS * CB]
        zsend[owner] = jnp.concatenate([part[:, :TD // 2], part[:, TD // 2:]], 0).astype(BF)
    lead_rows = jnp.concatenate([filt[pl.ds(0, 16)].astype(F32)[:CB], filt[pl.ds(K * CB, 16)].astype(F32)[:CB]], 0)
    leads[me_g] = lead_rows.astype(BF)
    zrecv[me_g] = zsend[me_g]

    def step_offset(i):
        return jnp.where(i % 2 == 1, (i + 1) // 2, NG - i // 2)

    def send_group(i, carry):
        dst = lax.rem(me_g + step_offset(i), NG)
        group_copy(leads.at[me_g], leads, ls, lr, dst, me_g).start()
        group_copy(zsend.at[dst], zrecv, zs, zr, dst, me_g).start()
        return carry

    lax.fori_loop(1, NG, send_group, 0)

    def correlate(src):
        lead_f[:, pl.ds(0, TD)] = leads[src].astype(F32)
        for row in range(STRIPES * CB):
            line = jnp.broadcast_to(lead_f[pl.ds(row, 1)], (R, KL))
            turned = pltpu.roll(line, 0, 1, stride=1, stride_axis=0)
            shifted[row // CB, pl.ds(row % CB * R, R)] = turned.astype(BF)
        halves = zrecv[src].astype(F32)
        width = SLOTS * CB
        padded = jnp.concatenate([halves[:width], halves[width:], jnp.zeros((width, QW - TD), F32)], 1)
        turns = [pltpu.roll(padded, MAXLAG - R * step, 1) for step in range(128 // R)]
        for slot in range(SLOTS):
            windows[slot] = jnp.concatenate([turn[slot * CB:(slot + 1) * CB] for turn in turns], 0).astype(BF)
        for slot in range(SLOTS):
            partner = jnp.concatenate(
                [windows[slot, :, pl.ds(128 * step, KL)] for step in range(1024 // 128)], 0
            )
            acc[slot] += lax.dot_general(
                partner, shifted[stripe_of[slot]], (((1,), (1,)), ((), ())), preferred_element_type=F32
            )

    correlate(me_g)

    def receive(i, carry):
        src = lax.rem(me_g + NG - step_offset(i), NG)
        group_copy(leads.at[me_g], leads, ls, lr, src, src).wait_recv()
        group_copy(zsend.at[src], zrecv, zs, zr, src, src).wait_recv()
        correlate(src)
        return carry

    lax.fori_loop(1, NG, receive, 0)

    scale = 1.0 / math.sqrt(TD)
    quarter = lax.broadcasted_iota(jnp.int32, (CB, 128), 1) // R

    def finish(slot, carry):
        for step in range(1024 // 128):
            for half in range(2):
                pieces = [
                    acc[slot, pl.ds(step * 4 * CB + s * CB, CB), pl.ds(half * 128, 128)] * scale
                    for s in range(4)
                ]
                for a in range(4):
                    value = pieces[a]
                    for s in range(4):
                        if s != a:
                            value = jnp.where(quarter == s, pltpu.roll(pieces[s], (s - a) * R % 128, 1), value)
                    width = min(128, LAGS - step * 128)
                    out_ref[slot, half * 4 + a, :, pl.ds(step * 128, width)] = value[:, :width]
        return carry

    lax.fori_loop(0, SLOTS, finish, 0)

    lax.fori_loop(1, NC, wait_first_sent, 0)

    def wait_packed_sent(d, carry):
        chan_copy(send_v, x_v, csend, crecv, lax.rem(me_c + d, NC), me_c).wait_send()
        return carry

    lax.fori_loop(1, NC, wait_packed_sent, 0)

    def wait_group_sent(i, carry):
        dst = lax.rem(me_g + step_offset(i), NG)
        group_copy(leads.at[me_g], leads, ls, lr, dst, me_g).wait_send()
        group_copy(zsend.at[dst], zrecv, zs, zr, dst, me_g).wait_send()
        return carry

    lax.fori_loop(1, NG, wait_group_sent, 0)


def local(raw_strain, whitening_taps, first_block, pair_owner):
    taps = jnp.pad(whitening_taps, (1, FW - TAPS - 1)).reshape(1, FW)
    vmem = pl.BlockSpec(memory_space=pltpu.VMEM)
    smem = pl.BlockSpec(memory_space=pltpu.SMEM)
    dma = pltpu.SemaphoreType.DMA
    return pl.pallas_call(
        kernel,
        out_shape=jax.ShapeDtypeStruct((SLOTS, CB, CB, LAGS), F32),
        in_specs=[pl.BlockSpec(memory_space=pl.ANY), vmem, smem, smem],
        out_specs=vmem,
        scratch_shapes=[
            pltpu.VMEM((ROWS, CHANNELS), F32),
            pltpu.VMEM((WIDE, ROWS), BF),
            pltpu.VMEM((NC, 8, 128), jnp.int32),
            pltpu.VMEM((1, 8, 128), jnp.int32),
            pltpu.VMEM((NC, ROWS, 128), BF),
            pltpu.VMEM((NC + 2, 128, ROWS), BF),
            pltpu.VMEM((128, TD), BF),
            pltpu.VMEM((NG, 2 * SLOTS * CB, TD // 2), BF),
            pltpu.VMEM((NG, 2 * SLOTS * CB, TD // 2), BF),
            pltpu.VMEM((NG, STRIPES * CB, TD), BF),
            pltpu.VMEM((STRIPES * CB, KL), F32),
            pltpu.VMEM((STRIPES, CB * R, KL), BF),
            pltpu.VMEM((SLOTS, 4 * CB, QW), BF),
            pltpu.VMEM((SLOTS, 256, 256), F32),
            dma, dma((NC,)), dma((NC,)), dma((NC,)), dma((NC,)),
            dma((NG,)), dma((NG,)), dma((NG,)), dma((NG,)),
        ],
        compiler_params=pltpu.CompilerParams(
            collective_id=0, has_side_effects=True, vmem_limit_bytes=56 << 20
        ),
        cost_estimate=pl.CostEstimate(flops=12 << 30, bytes_accessed=8 << 20, transcendentals=0),
    )(raw_strain, taps, first_block, pair_owner)


def solution(mesh):
    in_specs = (P(("tgroup", "chan"), None), P(), P("chan"), P("chan", None))
    out_specs = P(("tgroup", "chan"), None, None, None)
    return jax.shard_map(local, mesh=mesh, in_specs=in_specs, out_specs=out_specs, check_vma=False)
```

time: 783 us -> 93.7 us (0.12)
  local copies, waits for them, and re-layouts: 566 us -> 5.2 us
  waiting for transfers between devices: 157 us -> 0 us
  Pallas kernels: 0 us -> 87.4 us
  matrix products: 21.1 us -> 0 us
  between operations: 15.7 us -> 0.01 us
  starting transfers between devices: 10.1 us -> 0 us
    gather x808 -> x0, local copies, waits for them, and re-layouts: 523 us -> none
    unnamed x2 -> x0, waiting for transfers between devices: 127 us -> none
    pallas_call x0 -> x1, Pallas kernels: none -> 87.4 us  [local(): pl.pallas_call(kernel, out_shape=jax.ShapeDtypeStruct((SLOTS, CB, CB, LAG...]
    all_to_all x1 -> x0, waiting for transfers between devices: 26.3 us -> none  [local(): lax.all_to_all(grouped.astype(jnp.bfloat16), 'chan', split_axis=1, concat...]
    dot_general x5 -> x0, matrix products: 21.1 us -> none  [the longest x2 8.22 us: correlate(): jnp.einsum('raj,nbj->banr', shifted, windows, preferred_element_type=jnp....]
    unnamed x32 -> x2, local copies, waits for them, and re-layouts: 19.6 us -> 3.85 us
    reshape x7 -> x1, local copies, waits for them, and re-layouts: 11.2 us -> 0.6 us  [local(): taps = jnp.pad(whitening_taps, (1, FW - TAPS - 1)).reshape(1, FW)]
  transfers between devices with their start and end apart: 3 -> 0, of which waited for: 3 -> 0; matrix products, arithmetic and copies ran while one was open for 1% -> 0% of each run, Pallas kernels for 0% -> 0%
where the time goes in v1:
time: 93.7 us; the launch traced here: 92.7 us
  Pallas kernels  87.4 us (93%)
  local copies, waits for them, and re-layouts  5.2 us (6%)
    pallas_call x1, Pallas kernels, local(): pl.pallas_call(kernel, out_shape=jax.ShapeDtypeStruct((SLOTS, CB, CB, LAG...  87.4 us
    unnamed x2, local copies, waits for them, and re-layouts  3.85 us

profile of v1, /device:TPU:56, one launch (start us, length us, event | category | flops | bytes accessed | tf_op | source)
XLA Modules:
  0.0 92.7 jit_solution(7098599370082769596)
XLA Ops:
  0.0 0.8 pad.4
  0.8 0.6 reshape.3.taps_ref
  1.4 1.3 %copy.5.owner_ref = s32[16,1]{1,0:T(8,128)} copy(s32[16,1]{0,1:T(1,128)} %param.7) | data formatting | bytes 128 | tf_op args[3]
  2.7 87.4 %shard_map.46 = f32[5,8,8,1001]{3,2,1,0:T(8,128)} custom-call(f32[128,10240]{1,0:T(8,128)} %raw_ref.1, f32[1,768]{1,0:T(1,128)} %reshape.3.taps_ref, s32[2]{0:T(128)} %fb_ref.1, s32[16,1]{1,0:T(8,128)} %copy.5.owner_ref), custom_call_target="tpu_custom_call" | custom-call | flops 12884901888 | bytes 8388608 | tf_op jit(solution)/shard_map/pallas_call | solution.py:280
  90.1 2.5 %copy.7 = f32[5,8,8,1001]{3,2,1,0:T(8,128)} copy(f32[5,8,8,1001]{3,2,1,0:T(8,128)} %shard_map.46) | data formatting | bytes 2562560

commit v2 on v1

v2 whole, which is shorter than its diff:
```python
import math

import jax
import jax.numpy as jnp
from jax import lax
from jax.experimental import pallas as pl
from jax.experimental.pallas import tpu as pltpu
from jax.sharding import PartitionSpec as P

MESH = pl.DeviceIdType.MESH
MAXLAG = 500
LAGS = 1001
CB = 8
K = 8
STRIPES = 2
SLOTS = 5
TAPS = 255
NG = 8
NC = 32
CPD = 320
CHANNELS = 10240
ROWS = 128
TS = 4096
TD = 2048
HALF = TD // 2
PAIRS = STRIPES * K
WIDE = CHANNELS + 128
SPAN = 512
EARLY = 80
FB = 256
FW = 768
R = 32
KL = TD + 128
QW = TD + 1024
F32 = jnp.float32
BF = jnp.bfloat16
I32 = jnp.int32


def remote(src, dst, send_sem, recv_sem, axis, target):
    return pltpu.make_async_remote_copy(
        src_ref=src, dst_ref=dst, send_sem=send_sem, recv_sem=recv_sem,
        device_id={axis: target}, device_id_type=MESH,
    )


def kernel(
    raw_ref, taps_ref, fb_ref, owner_ref, acc,
    raw_v, raw_b, table_v, mine_v, send_v, x_v, filt, send0, recv0, send1, recv1, leads, lead_f, shifted, windows,
    raw_sem, fsend, frecv, asend, arecv, bsend, brecv, s0, r0, s1, r1, ls, lr,
):
    me_c = lax.axis_index("chan")
    me_g = lax.axis_index("tgroup")

    barrier = pltpu.get_barrier_semaphore()

    def greet_chan(d, carry):
        pl.semaphore_signal(barrier, inc=1, device_id={"chan": lax.rem(me_c + d, NC)}, device_id_type=MESH)
        return carry

    def greet_group(d, carry):
        pl.semaphore_signal(barrier, inc=1, device_id={"tgroup": lax.rem(me_g + d, NG)}, device_id_type=MESH)
        return carry

    lax.fori_loop(1, NC, greet_chan, 0)
    lax.fori_loop(1, NG, greet_group, 0)
    raw_in = pltpu.make_async_copy(raw_ref, raw_v, raw_sem)
    raw_in.start()

    owners = [owner_ref[q] for q in range(PAIRS)]
    slots = []
    for q in range(PAIRS):
        count = jnp.int32(0)
        for earlier in range(q):
            count = count + jnp.where(owners[earlier] == owners[q], 1, 0)
        slots.append(count)
    keys = [jnp.int32(q // K - 2) if q % K == 0 else slots[q] * PAIRS + q for q in range(PAIRS)]
    places = [jnp.int32(0)] * PAIRS
    for q in range(PAIRS):
        for other in range(q):
            ahead = jnp.where(keys[other] < keys[q], 1, 0)
            places[q] = places[q] + ahead
            places[other] = places[other] + 1 - ahead
    place_row = lax.broadcasted_iota(I32, (PAIRS, 128), 0)
    place_lane = lax.broadcasted_iota(I32, (1, 128), 1) // CB
    starts = jnp.zeros((PAIRS, 128), I32)
    target = jnp.zeros((1, 128), I32)
    for q in range(PAIRS):
        starts = jnp.where(place_row == places[q], (fb_ref[q // K] + q % K) * CB, starts)
        target = jnp.where(place_lane == places[q], owners[q] * SLOTS + slots[q], target)
    mine_v[...] = starts
    table_v[me_c] = starts
    stripe_of = []
    for s in range(SLOTS):
        value = jnp.int32(0)
        for q in range(K, PAIRS):
            value = value + jnp.where((owners[q] == me_g) & (slots[q] == s), 1, 0)
        stripe_of.append(value)

    raw_b[:, pl.ds(CHANNELS, 128)] = jnp.zeros((ROWS, 128), BF)
    x_v[0] = jnp.zeros((128, ROWS), BF)
    x_v[NC + 1] = jnp.zeros((128, ROWS), BF)
    lead_f[:, pl.ds(TD, 128)] = jnp.zeros((STRIPES * CB, 128), F32)

    pl.semaphore_wait(barrier, NC + NG - 2)

    def first_copy(d, peer, owner):
        return remote(mine_v, table_v.at[owner], fsend.at[d], frecv.at[d], "chan", peer)

    def send_first(d, carry):
        first_copy(d, lax.rem(me_c + d, NC), me_c).start()
        return carry

    lax.fori_loop(1, NC, send_first, 0)

    line = jnp.concatenate([taps_ref[...].reshape(1, TAPS), jnp.zeros((1, FW - TAPS), F32)], 1)
    band = pltpu.roll(jnp.broadcast_to(line, (FB, FW)), 1, 1, stride=2, stride_axis=0)
    band_hi = band.astype(BF)
    band_lo = (band - band_hi.astype(F32)).astype(BF)

    raw_in.wait()

    def round_raw(i, carry):
        at = pl.multiple_of(i * 512, 512)
        raw_b[:, pl.ds(at, 512)] = raw_v[:, pl.ds(at, 512)].astype(BF)
        return carry

    lax.fori_loop(0, CHANNELS // 512, round_raw, 0)

    def wait_first(d, carry):
        peer = lax.rem(me_c + NC - d, NC)
        first_copy(d, peer, peer).wait_recv()
        return carry

    lax.fori_loop(1, NC, wait_first, 0)

    ahead_by = lax.broadcasted_iota(I32, (CB, SPAN), 1) - lax.broadcasted_iota(I32, (CB, SPAN), 0)

    def packed(dst):
        base = (dst * CPD) // 128 * 128
        shift = dst * CPD - base
        hot = []
        for place in range(PAIRS):
            wanted = jnp.broadcast_to(table_v[dst, pl.ds(place, 1), :] + shift, (CB, 128))
            hot.append(jnp.where(ahead_by == jnp.concatenate([wanted] * (SPAN // 128), 1), 1.0, 0.0))
        chosen = jnp.concatenate(hot, 0).astype(BF)
        source = raw_b[:, pl.ds(pl.multiple_of(base, 128), SPAN)]
        return lax.dot_general(chosen, source, (((1,), (1,)), ((), ())), preferred_element_type=F32).astype(BF)

    def early_copy(d, dst, src):
        return remote(
            send_v.at[dst, pl.ds(0, EARLY)], x_v.at[1 + src, pl.ds(0, EARLY)], asend.at[d], arecv.at[d], "chan", dst
        )

    def late_copy(d, dst, src):
        return remote(
            send_v.at[dst, pl.ds(EARLY, 128 - EARLY)], x_v.at[1 + src, pl.ds(EARLY, 128 - EARLY)],
            bsend.at[d], brecv.at[d], "chan", dst,
        )

    def send_early(d, carry):
        dst = lax.rem(me_c + d, NC)
        send_v[dst] = packed(dst)
        early_copy(d, dst, me_c).start()
        return carry

    def send_late(d, carry):
        late_copy(d, lax.rem(me_c + d, NC), me_c).start()
        return carry

    lax.fori_loop(1, NC, send_early, 0)
    lax.fori_loop(1, NC, send_late, 0)
    x_v[1 + me_c] = packed(me_c)

    def wait_early(d, carry):
        peer = lax.rem(me_c + NC - d, NC)
        early_copy(d, peer, peer).wait_recv()
        return carry

    def wait_late(d, carry):
        peer = lax.rem(me_c + NC - d, NC)
        late_copy(d, peer, peer).wait_recv()
        return carry

    def whiten(at, count):
        window = jnp.concatenate(
            [
                jnp.concatenate([x_v[4 * block + part, pl.ds(at, count)] for part in range(FW // ROWS)], 1)
                for block in range(TD // FB)
            ],
            0,
        )
        y = sum(
            lax.dot_general(window, term, (((1,), (1,)), ((), ())), preferred_element_type=F32)
            for term in (band_hi, band_lo)
        )
        for block in range(TD // FB):
            filt[pl.ds(at, count), pl.ds(block * FB, FB)] = y[block * count:(block + 1) * count].astype(BF)

    def chosen_rows(first, count, depth):
        rows = NG * count * CB
        row_id = lax.broadcasted_iota(I32, (rows, depth), 0)
        col_id = lax.broadcasted_iota(I32, (rows, depth), 1)
        wanted = row_id // (count * CB) * SLOTS + first + row_id // CB % count
        pick = (jnp.broadcast_to(target[:, :depth], (rows, depth)) == wanted) & (row_id % CB == col_id % CB)
        rows_of = jnp.dot(
            jnp.where(pick, 1.0, 0.0).astype(BF), filt[pl.ds(0, depth)], preferred_element_type=F32
        )
        parts = [rows_of[o * count * CB:(o + 1) * count * CB] for o in range(NG)]
        return [jnp.concatenate([part[:, :HALF], part[:, HALF:]], 0).astype(BF) for part in parts]

    lax.fori_loop(1, NC, wait_early, 0)
    whiten(0, EARLY)

    right = lax.rem(me_g + 1, NG)
    left = lax.rem(me_g + NG - 1, NG)

    def lead_copy(way, hop):
        back = hop - 1 if way == 0 else NG - hop + 1
        origin = lax.rem(me_g + NG - back, NG)
        part = leads.at[origin] if hop < 4 else leads.at[origin, way]
        return remote(part, part, ls.at[way, hop - 1], lr.at[way, hop - 1], "tgroup", right if way == 0 else left)

    def lead_arrival(way, hop):
        back = hop if way == 0 else NG - hop
        origin = lax.rem(me_g + NG - back, NG)
        part = leads.at[origin] if hop < 4 else leads.at[origin, way]
        return remote(part, part, ls.at[way, hop - 1], lr.at[way, hop - 1], "tgroup", right if way == 0 else left)

    def pass_leads(hop):
        for way in range(2):
            lead_arrival(way, hop - 1).wait_recv()
            lead_copy(way, hop).start()

    for half in range(2):
        leads[me_g, half] = filt[pl.ds(0, STRIPES * CB), pl.ds(half * HALF, HALF)]
    for way in range(2):
        lead_copy(way, 1).start()

    def step_offset(i):
        return jnp.where(i % 2 == 1, (i + 1) // 2, NG - i // 2)

    def slot0_copy(i, dst, src):
        return remote(send0.at[dst], recv0.at[src], s0.at[i], r0.at[i], "tgroup", dst)

    def slot1_copy(i, dst, src):
        return remote(send1.at[dst], recv1.at[src], s1.at[i], r1.at[i], "tgroup", dst)

    def send_slot0(i, carry):
        slot0_copy(i, lax.rem(me_g + step_offset(i), NG), me_g).start()
        return carry

    def send_slot1(i, carry):
        slot1_copy(i, lax.rem(me_g + step_offset(i), NG), me_g).start()
        return carry

    for owner, part in enumerate(chosen_rows(0, 1, EARLY)):
        send0[owner] = part
    lax.fori_loop(1, NG, send_slot0, 0)
    recv0[me_g] = send0[me_g]

    def spread_leads(src):
        for half in range(2):
            lead_f[:, pl.ds(half * HALF, HALF)] = leads[src, half].astype(F32)
        for row in range(STRIPES * CB):
            line = jnp.broadcast_to(lead_f[pl.ds(row, 1)], (R, KL))
            turned = pltpu.roll(line, 0, 1, stride=1, stride_axis=0)
            shifted[row // CB, pl.ds(row % CB * R, R)] = turned.astype(BF)

    def correlate(halves, first, count, fresh=False):
        width = count * CB
        halves = halves.astype(F32)
        padded = jnp.concatenate([halves[:width], halves[width:], jnp.zeros((width, QW - TD), F32)], 1)
        turns = [pltpu.roll(padded, MAXLAG - R * step, 1) for step in range(128 // R)]
        for s in range(count):
            windows[first + s] = jnp.concatenate([turn[s * CB:(s + 1) * CB] for turn in turns], 0).astype(BF)
        for slot in range(first, first + count):
            partner = jnp.concatenate(
                [windows[slot, :, pl.ds(128 * step, KL)] for step in range(1024 // 128)], 0
            )
            product = lax.dot_general(
                partner, shifted[stripe_of[slot]], (((1,), (1,)), ((), ())), preferred_element_type=F32
            )
            acc[slot] = product if fresh else acc[slot] + product

    spread_leads(me_g)
    correlate(recv0[me_g], 0, 1, True)
    pass_leads(2)

    lax.fori_loop(1, NC, wait_late, 0)
    whiten(EARLY, 128 - EARLY)
    for owner, part in enumerate(chosen_rows(1, SLOTS - 1, 128)):
        send1[owner] = part
    pass_leads(3)
    lax.fori_loop(1, 5, send_slot1, 0)
    correlate(send1[me_g], 1, SLOTS - 1, True)
    pass_leads(4)
    lax.fori_loop(5, NG, send_slot1, 0)

    def receive(i, carry):
        src = lax.rem(me_g + NG - step_offset(i), NG)

        @pl.when(i == NG - 1)
        def _():
            for way in range(2):
                lead_arrival(way, 4).wait_recv()

        spread_leads(src)
        slot0_copy(i, src, src).wait_recv()
        slot1_copy(i, src, src).wait_recv()
        halves0 = recv0[src]
        halves1 = recv1[src]
        correlate(halves0, 0, 1)
        correlate(halves1, 1, SLOTS - 1)
        return carry

    lax.fori_loop(1, NG, receive, 0)

    def wait_chan_sent(d, carry):
        dst = lax.rem(me_c + d, NC)
        first_copy(d, dst, me_c).wait_send()
        early_copy(d, dst, me_c).wait_send()
        late_copy(d, dst, me_c).wait_send()
        return carry

    lax.fori_loop(1, NC, wait_chan_sent, 0)

    def wait_group_sent(i, carry):
        dst = lax.rem(me_g + step_offset(i), NG)
        slot0_copy(i, dst, me_g).wait_send()
        slot1_copy(i, dst, me_g).wait_send()
        return carry

    lax.fori_loop(1, NG, wait_group_sent, 0)
    for way in range(2):
        for hop in range(1, 5):
            lead_copy(way, hop).wait_send()


def finish(acc_ref, out_ref):
    scale = 1.0 / math.sqrt(TD)
    quarter = lax.broadcasted_iota(I32, (CB, 128), 1) // R
    for step in range(1024 // 128):
        for half in range(2):
            pieces = [
                acc_ref[0, pl.ds(step * 4 * CB + s * CB, CB), pl.ds(half * 128, 128)] * scale for s in range(4)
            ]
            for a in range(4):
                value = pieces[a]
                for s in range(4):
                    if s != a:
                        value = jnp.where(quarter == s, pltpu.roll(pieces[s], (s - a) * R % 128, 1), value)
                width = min(128, LAGS - step * 128)
                out_ref[0, half * 4 + a, :, pl.ds(step * 128, width)] = value[:, :width]


def local(raw_strain, whitening_taps, first_block, pair_owner):
    vmem = pl.BlockSpec(memory_space=pltpu.VMEM)
    smem = pl.BlockSpec(memory_space=pltpu.SMEM)
    dma = pltpu.SemaphoreType.DMA
    acc = pl.pallas_call(
        kernel,
        out_shape=jax.ShapeDtypeStruct((SLOTS, 256, 256), F32),
        in_specs=[pl.BlockSpec(memory_space=pl.ANY), vmem, smem, smem],
        out_specs=vmem,
        scratch_shapes=[
            pltpu.VMEM((ROWS, CHANNELS), F32),
            pltpu.VMEM((ROWS, WIDE), BF),
            pltpu.VMEM((NC, PAIRS, 128), I32),
            pltpu.VMEM((PAIRS, 128), I32),
            pltpu.VMEM((NC, 128, ROWS), BF),
            pltpu.VMEM((NC + 2, 128, ROWS), BF),
            pltpu.VMEM((128, TD), BF),
            pltpu.VMEM((NG, 2 * CB, HALF), BF),
            pltpu.VMEM((NG, 2 * CB, HALF), BF),
            pltpu.VMEM((NG, 2 * CB * (SLOTS - 1), HALF), BF),
            pltpu.VMEM((NG, 2 * CB * (SLOTS - 1), HALF), BF),
            pltpu.VMEM((NG, 2, STRIPES * CB, HALF), BF),
            pltpu.VMEM((STRIPES * CB, KL), F32),
            pltpu.VMEM((STRIPES, CB * R, KL), BF),
            pltpu.VMEM((SLOTS, 4 * CB, QW), BF),
            dma, dma((NC,)), dma((NC,)), dma((NC,)), dma((NC,)), dma((NC,)), dma((NC,)),
            dma((NG,)), dma((NG,)), dma((NG,)), dma((NG,)), dma((2, 4)), dma((2, 4)),
        ],
        compiler_params=pltpu.CompilerParams(
            collective_id=0, has_side_effects=True, vmem_limit_bytes=56 << 20
        ),
        cost_estimate=pl.CostEstimate(flops=12 << 30, bytes_accessed=8 << 20, transcendentals=0),
    )(raw_strain, whitening_taps, first_block, pair_owner.reshape(PAIRS))
    return pl.pallas_call(
        finish,
        grid=(SLOTS,),
        out_shape=jax.ShapeDtypeStruct((SLOTS, CB, CB, LAGS), F32),
        in_specs=[pl.BlockSpec((1, 256, 256), lambda s: (s, 0, 0))],
        out_specs=pl.BlockSpec((1, CB, CB, LAGS), lambda s: (s, 0, 0, 0)),
    )(acc)


def solution(mesh):
    in_specs = (P(("tgroup", "chan"), None), P(), P("chan"), P("chan", None))
    out_specs = P(("tgroup", "chan"), None, None, None)
    return jax.shard_map(local, mesh=mesh, in_specs=in_specs, out_specs=out_specs, check_vma=False)
```

time: 93.7 us -> 86 us (0.918)
  the two profiles are of different devices: /device:TPU:56 before, /device:TPU:14 now
where the time goes in v2:
time: 86 us; the launch traced here: 85.8 us
  Pallas kernels  85.8 us (100%)
    pallas_call x1, Pallas kernels, local(): pl.pallas_call(kernel, out_shape=jax.ShapeDtypeStruct((SLOTS, 256, 256),...  81.2 us
    pallas_call x1, Pallas kernels, local(): pl.pallas_call(finish, grid=(SLOTS,), out_shape=jax.ShapeDtypeStruct((SLO...  4.6 us

profile of v2, /device:TPU:14, one launch (start us, length us, event | category | flops | bytes accessed | tf_op | source)
XLA Modules:
  0.0 85.8 jit_solution(5832931688230284461)
XLA Ops:
  0.0 81.2 %shard_map.46.acc_ref = f32[5,256,256]{2,1,0:T(8,128)} custom-call(f32[128,10240]{1,0:T(8,128)} %raw_ref.1, f32[255]{0:T(256)} %taps_ref.1, s32[2]{0:T(128)} %fb_ref.1, s32[16]{0:T(128)} %bitcast.1), custom_call_target="tpu_custom_call" | custom-call | flops 12884901888 | bytes 8388608 | tf_op jit(solution)/shard_map/pallas_call | solution.py:361
  81.2 4.6 %shard_map.47 = f32[5,8,8,1001]{3,2,1,0:T(8,128)} custom-call(f32[5,256,256]{2,1,0:T(8,128)} %shard_map.46.acc_ref), custom_call_target="tpu_custom_call" | custom-call | tf_op jit(solution)/shard_map/pallas_call | solution.py:390

commit v3 on v2

--- a/solution.py
+++ b/solution.py
@@ -27,6 +27,9 @@
 WIDE = CHANNELS + 128
 SPAN = 512
 EARLY = 80
+PACK = 4
+AHEAD = 2
+IN_FLIGHT = 4
 FB = 256
 FW = 768
 R = 32
@@ -158,19 +161,25 @@
             bsend.at[d], brecv.at[d], "chan", dst,
         )
 
-    def send_early(d, carry):
-        dst = lax.rem(me_c + d, NC)
-        send_v[dst] = packed(dst)
-        early_copy(d, dst, me_c).start()
+    def send_early(i, carry):
+        dsts = [lax.rem(me_c + i * PACK + j, NC) for j in range(PACK)]
+        for dst, part in zip(dsts, [packed(dst) for dst in dsts]):
+            send_v[dst] = part
+        for j, dst in enumerate(dsts):
+
+            @pl.when(i * PACK + j > 0)
+            def _():
+                early_copy(i * PACK + j, dst, me_c).start()
+
         return carry
 
     def send_late(d, carry):
         late_copy(d, lax.rem(me_c + d, NC), me_c).start()
         return carry
 
-    lax.fori_loop(1, NC, send_early, 0)
+    lax.fori_loop(0, NC // PACK, send_early, 0)
     lax.fori_loop(1, NC, send_late, 0)
-    x_v[1 + me_c] = packed(me_c)
+    x_v[1 + me_c] = send_v[me_c]
 
     def wait_early(d, carry):
         peer = lax.rem(me_c + NC - d, NC)
@@ -265,9 +274,9 @@
         for row in range(STRIPES * CB):
             line = jnp.broadcast_to(lead_f[pl.ds(row, 1)], (R, KL))
             turned = pltpu.roll(line, 0, 1, stride=1, stride_axis=0)
-            shifted[row // CB, pl.ds(row % CB * R, R)] = turned.astype(BF)
-
-    def correlate(halves, first, count, fresh=False):
+            shifted[src, row // CB, pl.ds(row % CB * R, R)] = turned.astype(BF)
+
+    def correlate(src, halves, first, count, fresh=False):
         width = count * CB
         halves = halves.astype(F32)
         padded = jnp.concatenate([halves[:width], halves[width:], jnp.zeros((width, QW - TD), F32)], 1)
@@ -279,39 +288,60 @@
                 [windows[slot, :, pl.ds(128 * step, KL)] for step in range(1024 // 128)], 0
             )
             product = lax.dot_general(
-                partner, shifted[stripe_of[slot]], (((1,), (1,)), ((), ())), preferred_element_type=F32
+                partner, shifted[src, stripe_of[slot]], (((1,), (1,)), ((), ())), preferred_element_type=F32
             )
             acc[slot] = product if fresh else acc[slot] + product
 
     spread_leads(me_g)
-    correlate(recv0[me_g], 0, 1, True)
+    correlate(me_g, recv0[me_g], 0, 1, True)
     pass_leads(2)
+
+    def source(i):
+        return lax.rem(me_g + NG - step_offset(i), NG)
+
+    def first_pass(i):
+        src = source(i)
+        spread_leads(src)
+        slot0_copy(i, src, src).wait_recv()
+        correlate(src, recv0[src], 0, 1)
+
+    def ahead(i, carry):
+        first_pass(i)
+        return carry
+
+    lax.fori_loop(1, 1 + AHEAD, ahead, 0)
 
     lax.fori_loop(1, NC, wait_late, 0)
     whiten(EARLY, 128 - EARLY)
     for owner, part in enumerate(chosen_rows(1, SLOTS - 1, 128)):
         send1[owner] = part
+    lax.fori_loop(1, 3, send_slot1, 0)
     pass_leads(3)
-    lax.fori_loop(1, 5, send_slot1, 0)
-    correlate(send1[me_g], 1, SLOTS - 1, True)
-    pass_leads(4)
-    lax.fori_loop(5, NG, send_slot1, 0)
+    lax.fori_loop(3, 1 + IN_FLIGHT, send_slot1, 0)
+    correlate(me_g, send1[me_g], 1, SLOTS - 1, True)
 
     def receive(i, carry):
-        src = lax.rem(me_g + NG - step_offset(i), NG)
-
-        @pl.when(i == NG - 1)
+        @pl.when(i + AHEAD == 5)
+        def _():
+            pass_leads(4)
+
+        @pl.when(i + AHEAD == NG - 1)
         def _():
             for way in range(2):
                 lead_arrival(way, 4).wait_recv()
 
-        spread_leads(src)
-        slot0_copy(i, src, src).wait_recv()
+        @pl.when(i + AHEAD < NG)
+        def _():
+            first_pass(i + AHEAD)
+
+        src = source(i)
         slot1_copy(i, src, src).wait_recv()
-        halves0 = recv0[src]
-        halves1 = recv1[src]
-        correlate(halves0, 0, 1)
-        correlate(halves1, 1, SLOTS - 1)
+
+        @pl.when(i + IN_FLIGHT < NG)
+        def _():
+            send_slot1(i + IN_FLIGHT, 0)
+
+        correlate(src, recv1[src], 1, SLOTS - 1)
         return carry
 
     lax.fori_loop(1, NG, receive, 0)
@@ -337,21 +367,43 @@
             lead_copy(way, hop).wait_send()
 
 
-def finish(acc_ref, out_ref):
+def finish(acc_ref, out_ref, acc_v, out_v, in_sem, out_sem):
     scale = 1.0 / math.sqrt(TD)
-    quarter = lax.broadcasted_iota(I32, (CB, 128), 1) // R
-    for step in range(1024 // 128):
-        for half in range(2):
-            pieces = [
-                acc_ref[0, pl.ds(step * 4 * CB + s * CB, CB), pl.ds(half * 128, 128)] * scale for s in range(4)
-            ]
-            for a in range(4):
-                value = pieces[a]
-                for s in range(4):
-                    if s != a:
-                        value = jnp.where(quarter == s, pltpu.roll(pieces[s], (s - a) * R % 128, 1), value)
+    lane = lax.broadcasted_iota(I32, (CB, 128), 1)
+    low, even = lane < 64, lane // R % 2 == 0
+
+    def fetch(slot):
+        return pltpu.make_async_copy(acc_ref.at[slot], acc_v.at[slot], in_sem.at[slot])
+
+    def put(slot):
+        return pltpu.make_async_copy(out_v.at[slot], out_ref.at[slot], out_sem.at[slot])
+
+    for slot in range(SLOTS):
+        fetch(slot).start()
+
+    def one_slot(slot, carry):
+        fetch(slot).wait()
+        for step in range(1024 // 128):
+            for half in range(2):
+                p = [
+                    acc_v[slot, pl.ds(step * 4 * CB + s * CB, CB), pl.ds(half * 128, 128)] * scale for s in range(4)
+                ]
+                far = [None] * 4
+                for s in range(2):
+                    far[s] = jnp.where(low, p[s], pltpu.roll(p[s + 2], 64, 1))
+                    far[s + 2] = jnp.where(low, pltpu.roll(p[s], 64, 1), p[s + 2])
                 width = min(128, LAGS - step * 128)
-                out_ref[0, half * 4 + a, :, pl.ds(step * 128, width)] = value[:, :width]
+                for s in (0, 2):
+                    first = jnp.where(even, far[s], pltpu.roll(far[s + 1], R, 1))
+                    second = jnp.where(even, pltpu.roll(far[s], 128 - R, 1), far[s + 1])
+                    out_v[slot, half * 4 + s, :, pl.ds(step * 128, width)] = first[:, :width]
+                    out_v[slot, half * 4 + s + 1, :, pl.ds(step * 128, width)] = second[:, :width]
+        put(slot).start()
+        return carry
+
+    lax.fori_loop(0, SLOTS, one_slot, 0)
+    for slot in range(SLOTS):
+        put(slot).wait()
 
 
 def local(raw_strain, whitening_taps, first_block, pair_owner):
@@ -377,7 +429,7 @@
             pltpu.VMEM((NG, 2 * CB * (SLOTS - 1), HALF), BF),
             pltpu.VMEM((NG, 2, STRIPES * CB, HALF), BF),
             pltpu.VMEM((STRIPES * CB, KL), F32),
-            pltpu.VMEM((STRIPES, CB * R, KL), BF),
+            pltpu.VMEM((NG, STRIPES, CB * R, KL), BF),
             pltpu.VMEM((SLOTS, 4 * CB, QW), BF),
             dma, dma((NC,)), dma((NC,)), dma((NC,)), dma((NC,)), dma((NC,)), dma((NC,)),
             dma((NG,)), dma((NG,)), dma((NG,)), dma((NG,)), dma((2, 4)), dma((2, 4)),
@@ -389,10 +441,12 @@
     )(raw_strain, whitening_taps, first_block, pair_owner.reshape(PAIRS))
     return pl.pallas_call(
         finish,
-        grid=(SLOTS,),
         out_shape=jax.ShapeDtypeStruct((SLOTS, CB, CB, LAGS), F32),
-        in_specs=[pl.BlockSpec((1, 256, 256), lambda s: (s, 0, 0))],
-        out_specs=pl.BlockSpec((1, CB, CB, LAGS), lambda s: (s, 0, 0, 0)),
+        in_specs=[pl.BlockSpec(memory_space=pltpu.HBM)],
+        out_specs=pl.BlockSpec(memory_space=pltpu.HBM),
+        scratch_shapes=[
+            pltpu.VMEM((SLOTS, 256, 256), F32), pltpu.VMEM((SLOTS, CB, CB, LAGS), F32), dma((SLOTS,)), dma((SLOTS,)),
+        ],
     )(acc)
 
 

time: 86 us -> 78.8 us (0.916)
  the two profiles are of different devices: /device:TPU:14 before, /device:TPU:8 now
where the time goes in v3:
time: 78.8 us; the launch traced here: 78.7 us
  Pallas kernels  78.6 us (100%)
    pallas_call x1, Pallas kernels, local(): pl.pallas_call(kernel, out_shape=jax.ShapeDtypeStruct((SLOTS, 256, 256),...  75.6 us
    pallas_call x1, Pallas kernels, local(): pl.pallas_call(finish, out_shape=jax.ShapeDtypeStruct((SLOTS, CB, CB, LAG...  3.07 us

profile of v3, /device:TPU:8, one launch (start us, length us, event | category | flops | bytes accessed | tf_op | source)
XLA Modules:
  0.0 78.7 jit_solution(12935703608099466171)
XLA Ops:
  0.0 75.6 %shard_map.46.acc_ref = f32[5,256,256]{2,1,0:T(8,128)} custom-call(f32[128,10240]{1,0:T(8,128)} %raw_ref.1, f32[255]{0:T(256)} %taps_ref.1, s32[2]{0:T(128)} %fb_ref.1, s32[16]{0:T(128)} %bitcast.1), custom_call_target="tpu_custom_call" | custom-call | flops 12884901888 | bytes 8388608 | tf_op jit(solution)/shard_map/pallas_call | solution.py:413
  75.6 3.1 %shard_map.47 = f32[5,8,8,1001]{3,2,1,0:T(8,128)} custom-call(f32[5,256,256]{2,1,0:T(8,128)} %shard_map.46.acc_ref), custom_call_target="tpu_custom_call" | custom-call | tf_op jit(solution)/shard_map/pallas_call | solution.py:442

commit v4 on v3

--- a/solution.py
+++ b/solution.py
@@ -130,13 +130,6 @@
 
     lax.fori_loop(0, CHANNELS // 512, round_raw, 0)
 
-    def wait_first(d, carry):
-        peer = lax.rem(me_c + NC - d, NC)
-        first_copy(d, peer, peer).wait_recv()
-        return carry
-
-    lax.fori_loop(1, NC, wait_first, 0)
-
     ahead_by = lax.broadcasted_iota(I32, (CB, SPAN), 1) - lax.broadcasted_iota(I32, (CB, SPAN), 0)
 
     def packed(dst):
@@ -162,7 +155,13 @@
         )
 
     def send_early(i, carry):
-        dsts = [lax.rem(me_c + i * PACK + j, NC) for j in range(PACK)]
+        dsts = [lax.rem(me_c + NC - i * PACK - j, NC) for j in range(PACK)]
+        for j, dst in enumerate(dsts):
+
+            @pl.when(i * PACK + j > 0)
+            def _():
+                first_copy(i * PACK + j, dst, dst).wait_recv()
+
         for dst, part in zip(dsts, [packed(dst) for dst in dsts]):
             send_v[dst] = part
         for j, dst in enumerate(dsts):
@@ -174,7 +173,7 @@
         return carry
 
     def send_late(d, carry):
-        late_copy(d, lax.rem(me_c + d, NC), me_c).start()
+        late_copy(d, lax.rem(me_c + NC - d, NC), me_c).start()
         return carry
 
     lax.fori_loop(0, NC // PACK, send_early, 0)
@@ -182,12 +181,12 @@
     x_v[1 + me_c] = send_v[me_c]
 
     def wait_early(d, carry):
-        peer = lax.rem(me_c + NC - d, NC)
+        peer = lax.rem(me_c + d, NC)
         early_copy(d, peer, peer).wait_recv()
         return carry
 
     def wait_late(d, carry):
-        peer = lax.rem(me_c + NC - d, NC)
+        peer = lax.rem(me_c + d, NC)
         late_copy(d, peer, peer).wait_recv()
         return carry
 
@@ -347,10 +346,10 @@
     lax.fori_loop(1, NG, receive, 0)
 
     def wait_chan_sent(d, carry):
-        dst = lax.rem(me_c + d, NC)
+        dst, back = lax.rem(me_c + d, NC), lax.rem(me_c + NC - d, NC)
         first_copy(d, dst, me_c).wait_send()
-        early_copy(d, dst, me_c).wait_send()
-        late_copy(d, dst, me_c).wait_send()
+        early_copy(d, back, me_c).wait_send()
+        late_copy(d, back, me_c).wait_send()
         return carry
 
     lax.fori_loop(1, NC, wait_chan_sent, 0)

time: 78.8 us -> 75.4 us (0.957)
  the two profiles are of different devices: /device:TPU:8 before, /device:TPU:48 now
where the time goes in v4:
time: 75.4 us; the launch traced here: 75.3 us
  Pallas kernels  75.3 us (100%)
    pallas_call x1, Pallas kernels, local(): pl.pallas_call(kernel, out_shape=jax.ShapeDtypeStruct((SLOTS, 256, 256),...  72.2 us
    pallas_call x1, Pallas kernels, local(): pl.pallas_call(finish, out_shape=jax.ShapeDtypeStruct((SLOTS, CB, CB, LAG...  3.07 us

profile of v4, /device:TPU:48, one launch (start us, length us, event | category | flops | bytes accessed | tf_op | source)
XLA Modules:
  0.0 75.3 jit_solution(13374749881871466799)
XLA Ops:
  0.0 72.2 %shard_map.46.acc_ref = f32[5,256,256]{2,1,0:T(8,128)} custom-call(f32[128,10240]{1,0:T(8,128)} %raw_ref.1, f32[255]{0:T(256)} %taps_ref.1, s32[2]{0:T(128)} %fb_ref.1, s32[16]{0:T(128)} %bitcast.1), custom_call_target="tpu_custom_call" | custom-call | flops 12884901888 | bytes 8388608 | tf_op jit(solution)/shard_map/pallas_call | solution.py:412
  72.2 3.1 %shard_map.47 = f32[5,8,8,1001]{3,2,1,0:T(8,128)} custom-call(f32[5,256,256]{2,1,0:T(8,128)} %shard_map.46.acc_ref), custom_call_target="tpu_custom_call" | custom-call | tf_op jit(solution)/shard_map/pallas_call | solution.py:441

commit v5 on v4

--- a/solution.py
+++ b/solution.py
@@ -27,7 +27,7 @@
 WIDE = CHANNELS + 128
 SPAN = 512
 EARLY = 80
-PACK = 4
+PACK = 8
 AHEAD = 2
 IN_FLIGHT = 4
 FB = 256
@@ -91,6 +91,7 @@
     for q in range(PAIRS):
         starts = jnp.where(place_row == places[q], (fb_ref[q // K] + q % K) * CB, starts)
         target = jnp.where(place_lane == places[q], owners[q] * SLOTS + slots[q], target)
+    starts = jnp.where(lax.broadcasted_iota(I32, (CB, 128), 1) < 64, starts[:CB], starts[CB:])
     mine_v[...] = starts
     table_v[me_c] = starts
     stripe_of = []
@@ -132,12 +133,17 @@
 
     ahead_by = lax.broadcasted_iota(I32, (CB, SPAN), 1) - lax.broadcasted_iota(I32, (CB, SPAN), 0)
 
+    low = lax.broadcasted_iota(I32, (CB, 128), 1) < 64
+
     def packed(dst):
         base = (dst * CPD) // 128 * 128
         shift = dst * CPD - base
+        both = table_v[dst]
+        swapped = pltpu.roll(both, 64, 1)
+        rows = [jnp.where(low, both, swapped) + shift, jnp.where(low, swapped, both) + shift]
         hot = []
         for place in range(PAIRS):
-            wanted = jnp.broadcast_to(table_v[dst, pl.ds(place, 1), :] + shift, (CB, 128))
+            wanted = jnp.broadcast_to(rows[place // CB][place % CB:place % CB + 1], (CB, 128))
             hot.append(jnp.where(ahead_by == jnp.concatenate([wanted] * (SPAN // 128), 1), 1.0, 0.0))
         chosen = jnp.concatenate(hot, 0).astype(BF)
         source = raw_b[:, pl.ds(pl.multiple_of(base, 128), SPAN)]
@@ -417,8 +423,8 @@
         scratch_shapes=[
             pltpu.VMEM((ROWS, CHANNELS), F32),
             pltpu.VMEM((ROWS, WIDE), BF),
-            pltpu.VMEM((NC, PAIRS, 128), I32),
-            pltpu.VMEM((PAIRS, 128), I32),
+            pltpu.VMEM((NC, CB, 128), I32),
+            pltpu.VMEM((CB, 128), I32),
             pltpu.VMEM((NC, 128, ROWS), BF),
             pltpu.VMEM((NC + 2, 128, ROWS), BF),
             pltpu.VMEM((128, TD), BF),

time: 75.4 us -> 74.7 us (level)
  the two profiles are of different devices: /device:TPU:48 before, /device:TPU:56 now
where the time goes in v5:
time: 74.7 us; the launch traced here: 74.6 us
  Pallas kernels  74.6 us (100%)
    pallas_call x1, Pallas kernels, local(): pl.pallas_call(kernel, out_shape=jax.ShapeDtypeStruct((SLOTS, 256, 256),...  71.5 us
    pallas_call x1, Pallas kernels, local(): pl.pallas_call(finish, out_shape=jax.ShapeDtypeStruct((SLOTS, CB, CB, LAG...  3.07 us

profile of v5, /device:TPU:56, one launch (start us, length us, event | category | flops | bytes accessed | tf_op | source)
XLA Modules:
  0.0 74.6 jit_solution(9248904812361426481)
XLA Ops:
  0.0 71.5 %shard_map.46.acc_ref = f32[5,256,256]{2,1,0:T(8,128)} custom-call(f32[128,10240]{1,0:T(8,128)} %raw_ref.1, f32[255]{0:T(256)} %taps_ref.1, s32[2]{0:T(128)} %fb_ref.1, s32[16]{0:T(128)} %bitcast.1), custom_call_target="tpu_custom_call" | custom-call | flops 12884901888 | bytes 8388608 | tf_op jit(solution)/shard_map/pallas_call | solution.py:418
  71.5 3.1 %shard_map.47 = f32[5,8,8,1001]{3,2,1,0:T(8,128)} custom-call(f32[5,256,256]{2,1,0:T(8,128)} %shard_map.46.acc_ref), custom_call_target="tpu_custom_call" | custom-call | tf_op jit(solution)/shard_map/pallas_call | solution.py:447

commit v6 on v5

--- a/solution.py
+++ b/solution.py
@@ -27,7 +27,7 @@
 WIDE = CHANNELS + 128
 SPAN = 512
 EARLY = 80
-PACK = 8
+PACK = 4
 AHEAD = 2
 IN_FLIGHT = 4
 FB = 256

time: 74.7 us -> 73.7 us (0.987)
  Pallas kernels: 74.6 us -> 73.4 us
    pallas_call x1, Pallas kernels: 71.5 us -> 70.3 us  [local(): pl.pallas_call(kernel, out_shape=jax.ShapeDtypeStruct((SLOTS, 256, 256),...]
where the time goes in v6:
time: 73.7 us; the launch traced here: 73.4 us
  Pallas kernels  73.4 us (100%)
    pallas_call x1, Pallas kernels, local(): pl.pallas_call(kernel, out_shape=jax.ShapeDtypeStruct((SLOTS, 256, 256),...  70.3 us
    pallas_call x1, Pallas kernels, local(): pl.pallas_call(finish, out_shape=jax.ShapeDtypeStruct((SLOTS, CB, CB, LAG...  3.07 us

profile of v6, /device:TPU:56, one launch (start us, length us, event | category | flops | bytes accessed | tf_op | source)
XLA Modules:
  0.0 73.4 jit_solution(2788860755690262754)
XLA Ops:
  0.0 70.3 %shard_map.46.acc_ref = f32[5,256,256]{2,1,0:T(8,128)} custom-call(f32[128,10240]{1,0:T(8,128)} %raw_ref.1, f32[255]{0:T(256)} %taps_ref.1, s32[2]{0:T(128)} %fb_ref.1, s32[16]{0:T(128)} %bitcast.1), custom_call_target="tpu_custom_call" | custom-call | flops 12884901888 | bytes 8388608 | tf_op jit(solution)/shard_map/pallas_call | solution.py:418
  70.3 3.1 %shard_map.47 = f32[5,8,8,1001]{3,2,1,0:T(8,128)} custom-call(f32[5,256,256]{2,1,0:T(8,128)} %shard_map.46.acc_ref), custom_call_target="tpu_custom_call" | custom-call | tf_op jit(solution)/shard_map/pallas_call | solution.py:447
